TPU v7x, 256 devices: a whole 4x4x8 slice. The times are simulated.
256 devices in a mesh: tm: 8 (over z_hi, core), space: 32 (over y, x, z_lo).
Axes of the slice: x: 4, y: 4, z: 8 (z_hi: 4, z_lo: 2; z = z_hi * 2 + z_lo), core: 2. Of those that a mesh axis runs over, the one named last changes fastest.
Arguments:
- pressure: float32 [8, 2, 8, 512, 2048], P('tm', None, None, 'space'), may hold values from -6 to 6
- mobility: float32 [8, 2, 8, 512, 2048], P('tm', None, None, 'space'), may hold values from 0.05 to 1
- capacity: float32 [8, 2, 8, 512, 2048], P('tm', None, None, 'space'), may hold values from 0.5 to 2
- misfit_weight: float32 [8, 8, 512, 2048], P('tm', None, 'space'), may hold values from 0.2 to 1
- log_permeability: float32 [512, 2048], P('space'), may hold values from -3 to 3
- direction: float32 [512, 2048], P('space'), may hold values from -9 to 9
Outputs:
- hessian_product: float32 [512, 2048], P('space')
- curvature: float32 [], replicated
All inputs are finite; a program needn't handle non-finite values.
Results may differ from a plain program's by a relative error of at most 0.00002.
Values sent between devices are 32-bit elements; how exact they have to be, the bound alone decides.
A program may use at most 64 MiB of HBM per device.

v0:
```python
import jax
import jax.numpy as jnp
from jax import lax
from jax.sharding import PartitionSpec as P

LAYERS = 8
STEPS = 2


def extended(cells, sides, width):
    for axis, dim in sides:
        count = lax.axis_size(axis)
        ends = count - 1
        head = lax.slice_in_dim(cells, 0, width, axis=dim)
        tail = lax.slice_in_dim(cells, cells.shape[dim] - width, cells.shape[dim], axis=dim)
        cells = jnp.concatenate(
            [
                lax.ppermute(tail, axis, [(i, (i + 1) % count) for i in range(ends)]),
                cells,
                lax.ppermute(head, axis, [((i + 1) % count, i) for i in range(ends)]),
            ],
            axis=dim,
        )
    return cells


def shards(pressure, mobility, capacity, misfit_weight, log_permeability, direction):
    position = lax.axis_index("space")
    devices = lax.axis_size("space")
    height = pressure.shape[3]
    conduct = jnp.exp(log_permeability)
    scaled = conduct * direction
    pressure_w = pressure[0]
    mobility_w = mobility[0]
    capacity_w = capacity[0]
    weight_w = misfit_weight[0]
    face_y = (
        0.5
        * (mobility_w[..., 1:] + mobility_w[..., :-1])
        * (pressure_w[..., 1:] - pressure_w[..., :-1])
    )
    flux_y = 0.5 * (scaled[:, 1:] + scaled[:, :-1]) * face_y
    padded_y = jnp.pad(flux_y, ((0, 0), (0, 0), (0, 0), (1, 1)))
    change_y = padded_y[..., 1:] - padded_y[..., :-1]
    stacked = jnp.stack((pressure_w, mobility_w))
    padded = extended(stacked, (("space", 3),), 1)
    face_x = (
        0.5
        * (padded[1, ..., 1:, :] + padded[1, ..., :-1, :])
        * (padded[0, ..., 1:, :] - padded[0, ..., :-1, :])
    )
    face_index = lax.iota(jnp.int32, height + 1)
    keep_face = ((face_index > 0) | (position > 0)) & (
        (face_index < height) | (position < devices - 1)
    )
    face_x = face_x * keep_face.astype(jnp.float32)[:, None]
    scaled_ext = extended(scaled, (("space", 0),), 1)
    flux_x = 0.5 * (scaled_ext[1:] + scaled_ext[:-1]) * face_x
    change = flux_x[..., 1:, :] - flux_x[..., :-1, :] + change_y
    tangent = change / capacity_w
    adjoint = weight_w * tangent / capacity_w
    adjoint_ext = extended(adjoint, (("space", 2),), 1)
    term_x = face_x * (adjoint_ext[..., :-1, :] - adjoint_ext[..., 1:, :])
    summed_x = jnp.sum(term_x, axis=(0, 1))
    column_x = summed_x[1:] + summed_x[:-1]
    term_y = face_y * (adjoint[..., :-1] - adjoint[..., 1:])
    padded_ty = jnp.pad(term_y, ((0, 0), (0, 0), (0, 0), (1, 1)))
    column_y = jnp.sum(padded_ty[..., 1:] + padded_ty[..., :-1], axis=(0, 1))
    windows = lax.axis_size("tm")
    share = 0.5 * conduct * (column_x + column_y) / (LAYERS * STEPS * windows)
    hessian_product = lax.psum(share, "tm")
    cells = height * devices * direction.shape[1]
    curvature = lax.psum(jnp.sum(direction * hessian_product), "space") / cells
    return (hessian_product, curvature)


def solution(mesh):
    placed = (
        P("tm", None, None, "space", None),
        P("tm", None, None, "space", None),
        P("tm", None, None, "space", None),
        P("tm", None, "space", None),
        P("space", None),
        P("space", None),
    )
    return jax.shard_map(
        shards, mesh=mesh, in_specs=placed, out_specs=(P("space", None), P()), check_vma=False
    )
```

profile of v0, /device:TPU:0, one launch (start us, length us, event | category | flops | bytes accessed | tf_op | source)
XLA Modules:
  0.0 224.2 jit_solution(5592595358356381332)
XLA Ops:
  7.2 0.0 all-reduce.4.cloned.1.call-start
  7.2 0.0 copy-start.1
  7.2 1.1 exponential_multiply_fusion
  8.4 1.3 collective-permute-start.2
  9.7 4.5 %collective-permute-start.3 = (f32[1,2048]{1,0:T(1,128)S(1)}, f32[1,2048]{1,0:T(1,128)S(1)}, u32[]{:S(2)}, u32[]{:S(2)}) collective-permute-start(f32[1,2048]{1,0:T(1,128)S(1)} %get-tuple-element.10), channel_id=1, source_target_pairs={{0,1},{1,2},{2,3},{3,4},{4,5},{5,6},{6,7},{7,8},{8,9},{9,10},{10,1... | collective-permute-start | bytes 24584 | tf_op jit(solution)/shard_map/ppermute | solution.py:18
  14.2 1.7 constant_dynamic-update-slice_fusion.1
  16.0 0.0 copy-done.1
  16.0 0.0 copy-start
  16.0 0.2 constant_dynamic-update-slice_fusion
  16.2 0.0 copy-start.2
  16.2 1.9 copy-done.2
  18.2 0.4 fusion.27
  18.6 1.3 collective-permute-start
  19.9 4.6 %collective-permute-start.1 = (f32[2,2,8,1,2048]{4,3,2,1,0:T(1,128)S(1)}, f32[2,2,8,1,2048]{4,3,2,1,0:T(1,128)S(1)}, u32[]{:S(2)}, u32[]{:S(2)}) collective-permute-start(f32[2,2,8,1,2048]{4,3,2,1,0:T(1,128)S(1)} %get-tuple-element.7), channel_id=1, source_target_pairs={{0,1},{1,2},{2,3},{3,4},{4,5},{5,6},{6,7},{7,8},{8,9},{9,10},{10,1... | collective-permute-start | bytes 786440 | tf_op jit(solution)/shard_map/ppermute | solution.py:18
  24.5 0.1 fusion.24
  24.6 0.0 copy-done
  24.6 0.0 copy-start.3
  24.6 3.5 %broadcast_multiply_fusion.1 = (f32[2,8,16,2047]{3,2,1,0:T(8,128)S(1)}, f32[2,8,16,2047]{3,2,1,0:T(8,128)S(1)}) fusion(f32[16,2047]{1,0:T(8,128)S(1)} %fusion.24, f32[2,8,16,2048]{3,2,1,0:T(8,128)S(1)} %bitcast.10, f32[2,8,16,2048]{3,2,1,0:T(8,128)} %bitcast.11), kind=kLoop, calls=%fused_computation.36 | loop fusion | flops 2620160 | bytes 12707776 | tf_op jit(solution)/shard_map/mul | solution.py:42
  28.2 0.0 collective-permute-done.2
  28.2 0.0 collective-permute-done.3
  28.2 0.0 copy-start.4
  28.2 0.0 copy-start.5
  28.3 0.4 collective-permute-done
  28.6 0.0 collective-permute-done.1
  28.6 0.0 copy-done.3
  28.6 1.6 broadcast_multiply_fusion
  30.2 0.0 copy-done.4
  30.2 0.0 copy-done.5
  30.2 1.1 fusion.14
  31.4 0.2 fusion.28
  31.6 5.8 %collective-permute-start.4 = (f32[2,8,1,2048]{3,2,1,0:T(1,128)S(1)}, f32[2,8,1,2048]{3,2,1,0:T(1,128)S(1)}, u32[]{:S(2)}, u32[]{:S(2)}) collective-permute-start(f32[2,8,1,2048]{3,2,1,0:T(1,128)S(1)} %get-tuple-element.9), channel_id=1, source_target_pairs={{0,1},{1,2},{2,3},{3,4},{4,5},{5,6},{6,7},{7,8},{8,9},{9,10},{10,1... | collective-permute-start | bytes 393224 | tf_op jit(solution)/shard_map/ppermute | solution.py:18
  37.3 1.3 collective-permute-start.5
  38.6 0.8 fusion.17
  39.4 0.6 fusion.16
  40.1 0.0 collective-permute-done.4
  40.1 6.2 %collective-permute-done.5 = f32[2,8,1,2048]{3,2,1,0:T(1,128)S(1)} collective-permute-done((f32[2,8,1,2048]{3,2,1,0:T(1,128)S(1)}, f32[2,8,1,2048]{3,2,1,0:T(1,128)S(1)}, u32[]{:S(2)}, u32[]{:S(2)}) %collective-permute-start.5) | collective-permute-done | bytes 131104 | tf_op jit(solution)/shard_map/ppermute | solution.py:20
  46.2 0.0 copy-start.6
  46.2 0.0 copy-start.7
  46.2 0.8 fusion.9
  47.0 0.1 copy-done.6
  47.1 0.7 fusion.23
  47.8 0.0 all-reduce.4.cloned.1.call-update
  47.9 81.8 %all-reduce.4.cloned.1.call-done = f32[16,2048]{1,0:T(8,128)} async-done(((f32[16,2048]{1,0:T(8,128)}), f32[16,2048]{1,0:T(8,128)}) %all-reduce.4.cloned.1.call-update) | async-done | bytes 131088 | tf_op jit(solution)/shard_map/psum | solution.py:71
  129.7 0.0 copy-done.7
  129.7 1.5 multiply_reduce_fusion
  131.2 82.8 %psum.15 = f32[]{:T(128)} all-reduce(f32[]{:T(128)} %multiply_reduce_fusion), channel_id=1, replica_groups=mesh['tm'=8,'space'=32] {'space'}, use_global_device_ids=true, to_apply=%region_4.5 | all-reduce | flops 1 | bytes 8 | tf_op jit(solution)/shard_map/psum | solution.py:73
  214.7 1.6 copy.10
  (3 shorter events, 0.1 us)
Async XLA Ops:
  7.2 122.5 %all-reduce.4.cloned.1.call-start = ((), (), s32[]{:S(2)}) async-start(), calls=%async_computation | async-start | bytes 262144 | tf_op jit(solution)/shard_map/psum | solution.py:71
  7.2 8.8 %copy-start.1 = (f32[1,2,8,16,2048]{4,3,2,1,0:T(8,128)S(1)}, f32[1,2,8,16,2048]{4,3,2,1,0:T(8,128)}, u32[]{:S(2)}) copy-start(f32[1,2,8,16,2048]{4,3,2,1,0:T(8,128)} %param.7) | copy-start | bytes 6291460
  8.4 19.8 %collective-permute-start.2 = (f32[1,2048]{1,0:T(1,128)S(1)}, f32[1,2048]{1,0:T(1,128)S(1)}, u32[]{:S(2)}, u32[]{:S(2)}) collective-permute-start(f32[1,2048]{1,0:T(1,128)S(1)} %get-tuple-element.11), channel_id=1, source_target_pairs={{1,0},{2,1},{3,2},{4,3},{5,4},{6,5},{7,6},{8,7},{9,8},{10,9},{11,1... | collective-permute-start | bytes 24584 | tf_op jit(solution)/shard_map/ppermute | solution.py:20
  9.7 18.5 %collective-permute-start.3 = (f32[1,2048]{1,0:T(1,128)S(1)}, f32[1,2048]{1,0:T(1,128)S(1)}, u32[]{:S(2)}, u32[]{:S(2)}) collective-permute-start(f32[1,2048]{1,0:T(1,128)S(1)} %get-tuple-element.10), channel_id=1, source_target_pairs={{0,1},{1,2},{2,3},{3,4},{4,5},{5,6},{6,7},{7,8},{8,9},{9,10},{10,1... | collective-permute-start | bytes 24584 | tf_op jit(solution)/shard_map/ppermute | solution.py:18
  16.0 8.6 %copy-start = (f32[1,2,8,16,2048]{4,3,2,1,0:T(8,128)S(1)}, f32[1,2,8,16,2048]{4,3,2,1,0:T(8,128)}, u32[]{:S(2)}) copy-start(f32[1,2,8,16,2048]{4,3,2,1,0:T(8,128)} %param.6) | copy-start | bytes 6291460
  16.2 1.9 copy-start.2
  18.6 10.0 %collective-permute-start = (f32[2,2,8,1,2048]{4,3,2,1,0:T(1,128)S(1)}, f32[2,2,8,1,2048]{4,3,2,1,0:T(1,128)S(1)}, u32[]{:S(2)}, u32[]{:S(2)}) collective-permute-start(f32[2,2,8,1,2048]{4,3,2,1,0:T(1,128)S(1)} %get-tuple-element.6), channel_id=1, source_target_pairs={{1,0},{2,1},{3,2},{4,3},{5,4},{6,5},{7,6},{8,7},{9,8},{10,9},{11,1... | collective-permute-start | bytes 786440 | tf_op jit(solution)/shard_map/ppermute | solution.py:20
  19.9 8.7 %collective-permute-start.1 = (f32[2,2,8,1,2048]{4,3,2,1,0:T(1,128)S(1)}, f32[2,2,8,1,2048]{4,3,2,1,0:T(1,128)S(1)}, u32[]{:S(2)}, u32[]{:S(2)}) collective-permute-start(f32[2,2,8,1,2048]{4,3,2,1,0:T(1,128)S(1)} %get-tuple-element.7), channel_id=1, source_target_pairs={{0,1},{1,2},{2,3},{3,4},{4,5},{5,6},{6,7},{7,8},{8,9},{9,10},{10,1... | collective-permute-start | bytes 786440 | tf_op jit(solution)/shard_map/ppermute | solution.py:18
  24.6 4.0 %copy-start.3 = (f32[2,2,8,16,2048]{4,3,2,1,0:T(8,128)S(1)}, f32[2,2,8,16,2048]{4,3,2,1,0:T(8,128)}, u32[]{:S(2)}) copy-start(f32[2,2,8,16,2048]{4,3,2,1,0:T(8,128)} %copy-done.2) | copy-start | bytes 12582916
  28.2 2.0 copy-start.4
  28.2 2.0 copy-start.5
  31.6 8.5 %collective-permute-start.4 = (f32[2,8,1,2048]{3,2,1,0:T(1,128)S(1)}, f32[2,8,1,2048]{3,2,1,0:T(1,128)S(1)}, u32[]{:S(2)}, u32[]{:S(2)}) collective-permute-start(f32[2,8,1,2048]{3,2,1,0:T(1,128)S(1)} %get-tuple-element.9), channel_id=1, source_target_pairs={{0,1},{1,2},{2,3},{3,4},{4,5},{5,6},{6,7},{7,8},{8,9},{9,10},{10,1... | collective-permute-start | bytes 393224 | tf_op jit(solution)/shard_map/ppermute | solution.py:18
  37.3 8.9 %collective-permute-start.5 = (f32[2,8,1,2048]{3,2,1,0:T(1,128)S(1)}, f32[2,8,1,2048]{3,2,1,0:T(1,128)S(1)}, u32[]{:S(2)}, u32[]{:S(2)}) collective-permute-start(f32[2,8,1,2048]{3,2,1,0:T(1,128)S(1)} %get-tuple-element.8), channel_id=1, source_target_pairs={{1,0},{2,1},{3,2},{4,3},{5,4},{6,5},{7,6},{8,7},{9,8},{10,9},{11,1... | collective-permute-start | bytes 393224 | tf_op jit(solution)/shard_map/ppermute | solution.py:20
  46.2 0.9 copy-start.6
  46.2 83.5 %copy-start.7 = (f32[16,2048]{1,0:T(8,128)S(1)}, f32[16,2048]{1,0:T(8,128)}, u32[]{:S(2)}) copy-start(f32[16,2048]{1,0:T(8,128)} %param.11) | copy-start | bytes 393220
Sparse Core Ops, SparseCore 0:
  48.0 81.6 all-reduce.3
where the time goes:
time: 225 us; the launch traced here: 224 us
  waiting for transfers between devices  88.4 us (39%)
  blocking collectives  82.8 us (37%)
  starting transfers between devices  18.8 us (8%)
  between operations  16.1 us (7%)
  other arithmetic  12 us (5%)
  local copies, waits for them, and re-layouts  6.22 us (3%)
    psum x1, blocking collectives, shards(): curvature = lax.psum(jnp.sum(direction * hessian_product), 'space') / cells  82.8 us
    psum x1, waiting for transfers between devices, shards(): hessian_product = lax.psum(share, 'tm')  81.8 us
    ppermute x3, starting transfers between devices, extended(): lax.ppermute(tail, axis, [(i, (i + 1) % count) for i in range(ends)])  14.9 us
    ppermute x3, waiting for transfers between devices, extended(): lax.ppermute(head, axis, [((i + 1) % count, i) for i in range(ends)])  6.54 us
    unnamed x18, local copies, waits for them, and re-layouts  5.38 us
  transfers between devices with their start and end apart: 7, of which 3 were waited for; matrix products, arithmetic and copies ran while one was open for 3% of the time, Pallas kernels for 0%

commit v1 on v0

--- a/solution.py
+++ b/solution.py
@@ -68,7 +68,8 @@
     column_y = jnp.sum(padded_ty[..., 1:] + padded_ty[..., :-1], axis=(0, 1))
     windows = lax.axis_size("tm")
     share = 0.5 * conduct * (column_x + column_y) / (LAYERS * STEPS * windows)
-    hessian_product = lax.psum(share, "tm")
+    parts = lax.all_gather(share, "tm", axis=0, tiled=False)
+    hessian_product = parts.sum(axis=0)
     cells = height * devices * direction.shape[1]
     curvature = lax.psum(jnp.sum(direction * hessian_product), "space") / cells
     return (hessian_product, curvature)

time: 225 us -> 182 us (0.81)
  waiting for transfers between devices: 88.4 us -> 46.4 us
    psum x1 -> x0, waiting for transfers between devices: 81.8 us -> none  [shards(): hessian_product = lax.psum(share, 'tm')]
    all_gather x0 -> x1, waiting for transfers between devices: none -> 39.9 us  [shards(): parts = lax.all_gather(share, 'tm', axis=0, tiled=False)]
    unnamed x18 -> x19, local copies, waits for them, and re-layouts: 5.38 us -> 3.87 us
  transfers between devices with their start and end apart: 7 -> 7, of which waited for: 3 -> 3; matrix products, arithmetic and copies ran while one was open for 3% -> 4% of each run, Pallas kernels for 0% -> 0%
where the time goes in v1:
time: 182 us; the launch traced here: 181 us
  blocking collectives  82.9 us (46%)
  waiting for transfers between devices  46.4 us (25%)
  starting transfers between devices  18.8 us (10%)
  between operations  16.1 us (9%)
  other arithmetic  12.3 us (7%)
  local copies, waits for them, and re-layouts  4.72 us (3%)
    psum x1, blocking collectives, shards(): curvature = lax.psum(jnp.sum(direction * hessian_product), 'space') / cells  82.9 us
    all_gather x1, waiting for transfers between devices, shards(): parts = lax.all_gather(share, 'tm', axis=0, tiled=False)  39.9 us
    ppermute x3, starting transfers between devices, extended(): lax.ppermute(tail, axis, [(i, (i + 1) % count) for i in range(ends)])  14.9 us
    ppermute x3, waiting for transfers between devices, extended(): lax.ppermute(head, axis, [((i + 1) % count, i) for i in range(ends)])  6.54 us
    ppermute x3, starting transfers between devices, extended(): lax.ppermute(head, axis, [((i + 1) % count, i) for i in range(ends)])  3.88 us
    unnamed x19, local copies, waits for them, and re-layouts  3.87 us
  transfers between devices with their start and end apart: 7, of which 3 were waited for; matrix products, arithmetic and copies ran while one was open for 4% of the time, Pallas kernels for 0%

profile of v1, /device:TPU:0, one launch (start us, length us, event | category | flops | bytes accessed | tf_op | source)
XLA Modules:
  0.0 181.2 jit_solution(11701703171048602270)
XLA Ops:
  7.2 0.0 all-gather.3.cloned.1.call-start
  7.2 0.0 copy-start.1
  7.2 1.1 exponential_multiply_fusion
  8.4 1.3 collective-permute-start.2
  9.7 4.5 %collective-permute-start.3 = (f32[1,2048]{1,0:T(1,128)S(1)}, f32[1,2048]{1,0:T(1,128)S(1)}, u32[]{:S(2)}, u32[]{:S(2)}) collective-permute-start(f32[1,2048]{1,0:T(1,128)S(1)} %get-tuple-element.10), channel_id=1, source_target_pairs={{0,1},{1,2},{2,3},{3,4},{4,5},{5,6},{6,7},{7,8},{8,9},{9,10},{10,1... | collective-permute-start | bytes 24584 | tf_op jit(solution)/shard_map/ppermute | solution.py:18
  14.2 1.7 constant_dynamic-update-slice_fusion.1
  16.0 0.0 copy-done.1
  16.0 0.0 copy-start
  16.0 0.2 constant_dynamic-update-slice_fusion
  16.2 0.0 copy-start.2
  16.2 1.9 %copy-done.2 = f32[2,2,8,16,2048]{4,3,2,1,0:T(8,128)} copy-done((f32[2,2,8,16,2048]{4,3,2,1,0:T(8,128)}, f32[2,2,8,16,2048]{4,3,2,1,0:T(8,128)S(1)}, u32[]{:S(2)}) %copy-start.2) | copy-done | bytes 4194328
  18.2 0.4 fusion.27
  18.6 1.3 collective-permute-start
  19.9 4.6 %collective-permute-start.1 = (f32[2,2,8,1,2048]{4,3,2,1,0:T(1,128)S(1)}, f32[2,2,8,1,2048]{4,3,2,1,0:T(1,128)S(1)}, u32[]{:S(2)}, u32[]{:S(2)}) collective-permute-start(f32[2,2,8,1,2048]{4,3,2,1,0:T(1,128)S(1)} %get-tuple-element.7), channel_id=1, source_target_pairs={{0,1},{1,2},{2,3},{3,4},{4,5},{5,6},{6,7},{7,8},{8,9},{9,10},{10,1... | collective-permute-start | bytes 786440 | tf_op jit(solution)/shard_map/ppermute | solution.py:18
  24.5 0.1 fusion.24
  24.6 0.0 copy-done
  24.6 0.0 copy-start.3
  24.6 3.5 %broadcast_multiply_fusion.1 = (f32[2,8,16,2047]{3,2,1,0:T(8,128)S(1)}, f32[2,8,16,2047]{3,2,1,0:T(8,128)S(1)}) fusion(f32[16,2047]{1,0:T(8,128)S(1)} %fusion.24, f32[2,8,16,2048]{3,2,1,0:T(8,128)S(1)} %bitcast.11, f32[2,8,16,2048]{3,2,1,0:T(8,128)} %bitcast.12), kind=kLoop, calls=%fused_computation.36 | loop fusion | flops 2620160 | bytes 12707776 | tf_op jit(solution)/shard_map/mul | solution.py:42
  28.2 0.0 collective-permute-done.2
  28.2 0.0 collective-permute-done.3
  28.2 0.0 copy-start.4
  28.2 0.0 copy-start.5
  28.3 0.4 collective-permute-done
  28.6 0.0 collective-permute-done.1
  28.6 0.0 copy-done.3
  28.6 1.6 broadcast_multiply_fusion
  30.2 0.0 copy-done.4
  30.2 0.0 copy-done.5
  30.2 1.1 fusion.14
  31.4 0.2 fusion.28
  31.6 5.8 %collective-permute-start.4 = (f32[2,8,1,2048]{3,2,1,0:T(1,128)S(1)}, f32[2,8,1,2048]{3,2,1,0:T(1,128)S(1)}, u32[]{:S(2)}, u32[]{:S(2)}) collective-permute-start(f32[2,8,1,2048]{3,2,1,0:T(1,128)S(1)} %get-tuple-element.9), channel_id=1, source_target_pairs={{0,1},{1,2},{2,3},{3,4},{4,5},{5,6},{6,7},{7,8},{8,9},{9,10},{10,1... | collective-permute-start | bytes 393224 | tf_op jit(solution)/shard_map/ppermute | solution.py:18
  37.3 1.3 collective-permute-start.5
  38.6 0.8 fusion.17
  39.4 0.6 fusion.16
  40.1 0.0 collective-permute-done.4
  40.1 6.2 %collective-permute-done.5 = f32[2,8,1,2048]{3,2,1,0:T(1,128)S(1)} collective-permute-done((f32[2,8,1,2048]{3,2,1,0:T(1,128)S(1)}, f32[2,8,1,2048]{3,2,1,0:T(1,128)S(1)}, u32[]{:S(2)}, u32[]{:S(2)}) %collective-permute-start.5) | collective-permute-done | bytes 131104 | tf_op jit(solution)/shard_map/ppermute | solution.py:20
  46.2 0.0 copy-start.6
  46.2 0.7 fusion.9
  47.0 0.2 copy-done.6
  47.1 0.7 fusion.23
  47.8 0.0 all-gather.3.cloned.1.call-update
  47.9 39.9 %all-gather.3.cloned.1.call-done = f32[128,2048]{1,0:T(8,128)} async-done(((f32[16,2048]{1,0:T(8,128)}), f32[128,2048]{1,0:T(8,128)}) %all-gather.3.cloned.1.call-update) | async-done | bytes 1048592 | tf_op jit(solution)/shard_map/all_gather | solution.py:71
  87.7 1.3 reduce_sum.38
  89.0 0.0 copy-done.7
  89.0 0.0 copy-start.8
  89.0 0.6 multiply_reduce_fusion
  89.7 82.9 %psum.7 = f32[]{:T(128)} all-reduce(f32[]{:T(128)} %multiply_reduce_fusion), channel_id=1, replica_groups=mesh['tm'=8,'space'=32] {'space'}, use_global_device_ids=true, to_apply=%region_4.5 | all-reduce | flops 1 | bytes 8 | tf_op jit(solution)/shard_map/psum | solution.py:74
  173.2 0.0 copy-done.8
  (4 shorter events, 0.1 us)
Async XLA Ops:
  7.2 80.6 %all-gather.3.cloned.1.call-start = ((), (), s32[]{:S(2)}) async-start(), calls=%async_computation | async-start | bytes 1179648 | tf_op jit(solution)/shard_map/all_gather | solution.py:71
  7.2 8.8 %copy-start.1 = (f32[1,2,8,16,2048]{4,3,2,1,0:T(8,128)S(1)}, f32[1,2,8,16,2048]{4,3,2,1,0:T(8,128)}, u32[]{:S(2)}) copy-start(f32[1,2,8,16,2048]{4,3,2,1,0:T(8,128)} %param.7) | copy-start | bytes 6291460
  8.4 19.8 %collective-permute-start.2 = (f32[1,2048]{1,0:T(1,128)S(1)}, f32[1,2048]{1,0:T(1,128)S(1)}, u32[]{:S(2)}, u32[]{:S(2)}) collective-permute-start(f32[1,2048]{1,0:T(1,128)S(1)} %get-tuple-element.11), channel_id=1, source_target_pairs={{1,0},{2,1},{3,2},{4,3},{5,4},{6,5},{7,6},{8,7},{9,8},{10,9},{11,1... | collective-permute-start | bytes 24584 | tf_op jit(solution)/shard_map/ppermute | solution.py:20
  9.7 18.5 %collective-permute-start.3 = (f32[1,2048]{1,0:T(1,128)S(1)}, f32[1,2048]{1,0:T(1,128)S(1)}, u32[]{:S(2)}, u32[]{:S(2)}) collective-permute-start(f32[1,2048]{1,0:T(1,128)S(1)} %get-tuple-element.10), channel_id=1, source_target_pairs={{0,1},{1,2},{2,3},{3,4},{4,5},{5,6},{6,7},{7,8},{8,9},{9,10},{10,1... | collective-permute-start | bytes 24584 | tf_op jit(solution)/shard_map/ppermute | solution.py:18
  16.0 8.6 %copy-start = (f32[1,2,8,16,2048]{4,3,2,1,0:T(8,128)S(1)}, f32[1,2,8,16,2048]{4,3,2,1,0:T(8,128)}, u32[]{:S(2)}) copy-start(f32[1,2,8,16,2048]{4,3,2,1,0:T(8,128)} %param.6) | copy-start | bytes 6291460
  16.2 1.9 %copy-start.2 = (f32[2,2,8,16,2048]{4,3,2,1,0:T(8,128)}, f32[2,2,8,16,2048]{4,3,2,1,0:T(8,128)S(1)}, u32[]{:S(2)}) copy-start(f32[2,2,8,16,2048]{4,3,2,1,0:T(8,128)S(1)} %constant_dynamic-update-slice_fusion) | copy-start | bytes 12582916
  18.6 10.0 %collective-permute-start = (f32[2,2,8,1,2048]{4,3,2,1,0:T(1,128)S(1)}, f32[2,2,8,1,2048]{4,3,2,1,0:T(1,128)S(1)}, u32[]{:S(2)}, u32[]{:S(2)}) collective-permute-start(f32[2,2,8,1,2048]{4,3,2,1,0:T(1,128)S(1)} %get-tuple-element.6), channel_id=1, source_target_pairs={{1,0},{2,1},{3,2},{4,3},{5,4},{6,5},{7,6},{8,7},{9,8},{10,9},{11,1... | collective-permute-start | bytes 786440 | tf_op jit(solution)/shard_map/ppermute | solution.py:20
  19.9 8.7 %collective-permute-start.1 = (f32[2,2,8,1,2048]{4,3,2,1,0:T(1,128)S(1)}, f32[2,2,8,1,2048]{4,3,2,1,0:T(1,128)S(1)}, u32[]{:S(2)}, u32[]{:S(2)}) collective-permute-start(f32[2,2,8,1,2048]{4,3,2,1,0:T(1,128)S(1)} %get-tuple-element.7), channel_id=1, source_target_pairs={{0,1},{1,2},{2,3},{3,4},{4,5},{5,6},{6,7},{7,8},{8,9},{9,10},{10,1... | collective-permute-start | bytes 786440 | tf_op jit(solution)/shard_map/ppermute | solution.py:18
  24.6 4.0 %copy-start.3 = (f32[2,2,8,16,2048]{4,3,2,1,0:T(8,128)S(1)}, f32[2,2,8,16,2048]{4,3,2,1,0:T(8,128)}, u32[]{:S(2)}) copy-start(f32[2,2,8,16,2048]{4,3,2,1,0:T(8,128)} %copy-done.2) | copy-start | bytes 12582916
  28.2 2.0 %copy-start.4 = (f32[1,2,8,16,2048]{4,3,2,1,0:T(8,128)S(1)}, f32[1,2,8,16,2048]{4,3,2,1,0:T(8,128)}, u32[]{:S(2)}) copy-start(f32[1,2,8,16,2048]{4,3,2,1,0:T(8,128)} %param.8) | copy-start | bytes 6291460
  28.2 2.0 %copy-start.5 = (f32[1,8,16,2048]{3,2,1,0:T(8,128)S(1)}, f32[1,8,16,2048]{3,2,1,0:T(8,128)}, u32[]{:S(2)}) copy-start(f32[1,8,16,2048]{3,2,1,0:T(8,128)} %param.9) | copy-start | bytes 3145732
  31.6 8.5 %collective-permute-start.4 = (f32[2,8,1,2048]{3,2,1,0:T(1,128)S(1)}, f32[2,8,1,2048]{3,2,1,0:T(1,128)S(1)}, u32[]{:S(2)}, u32[]{:S(2)}) collective-permute-start(f32[2,8,1,2048]{3,2,1,0:T(1,128)S(1)} %get-tuple-element.9), channel_id=1, source_target_pairs={{0,1},{1,2},{2,3},{3,4},{4,5},{5,6},{6,7},{7,8},{8,9},{9,10},{10,1... | collective-permute-start | bytes 393224 | tf_op jit(solution)/shard_map/ppermute | solution.py:18
  37.3 8.9 %collective-permute-start.5 = (f32[2,8,1,2048]{3,2,1,0:T(1,128)S(1)}, f32[2,8,1,2048]{3,2,1,0:T(1,128)S(1)}, u32[]{:S(2)}, u32[]{:S(2)}) collective-permute-start(f32[2,8,1,2048]{3,2,1,0:T(1,128)S(1)} %get-tuple-element.8), channel_id=1, source_target_pairs={{1,0},{2,1},{3,2},{4,3},{5,4},{6,5},{7,6},{8,7},{9,8},{10,9},{11,1... | collective-permute-start | bytes 393224 | tf_op jit(solution)/shard_map/ppermute | solution.py:20
  46.2 0.9 copy-start.6
  46.2 42.8 %copy-start.7 = (f32[16,2048]{1,0:T(8,128)S(1)}, f32[16,2048]{1,0:T(8,128)}, u32[]{:S(2)}) copy-start(f32[16,2048]{1,0:T(8,128)} %param.11) | copy-start | bytes 393220
  89.0 84.2 %copy-start.8 = (f32[16,2048]{1,0:T(8,128)}, f32[16,2048]{1,0:T(8,128)S(1)}, u32[]{:S(2)}) copy-start(f32[16,2048]{1,0:T(8,128)S(1)} %reduce_sum.38) | copy-start | bytes 393220
Sparse Core Ops, SparseCore 0:
  48.0 39.7 all-gather.2
